TPU v7x, 256 devices: a whole 4x4x8 slice. The times are simulated.
256 devices in a mesh: dp: 4 (over x), fsdp: 64 (over z, y, core).
Axes of the slice: x: 4, y: 4, z: 8, core: 2. Of those that a mesh axis runs over, the one named last changes fastest.
Arguments:
- inputs: bfloat16 [512, 16384], P('dp', 'fsdp'), may hold values from -140 to 140
- norm_gain_vector: bfloat16 [16384], P('fsdp'), may hold values from 0.5 to 1.5
- weight: bfloat16 [16384, 16384], P(None, 'fsdp'), may hold values from -0.046875 to 0.046875
- down_adapters: bfloat16 [16384, 16, 32], P('fsdp'), may hold values from -0.046875 to 0.046875
- up_adapters: bfloat16 [16, 32, 16384], P(None, None, 'fsdp'), may hold values from -1 to 1
- tenant: int32 [512], P('dp'), may hold values from 0 to 15
- tenant_slot_index: int32 [16], replicated, may hold values from 0 to 31, as said below
- live_row_count: int32 [4], P('dp'), may hold values from 1 to 128, 320 in all
- cotangent: bfloat16 [512, 16384], P('dp', 'fsdp'), may hold values from -6 to 6
- down_row_factor: float32 [32, 16384], P('dp', 'fsdp'), may hold values from 300 to 30000
- down_column_factor: float32 [32, 32], P('dp'), may hold values from 300 to 30000
- up_row_factor: float32 [32, 32], P('dp'), may hold values from 0.5 to 50
- up_column_factor: float32 [32, 16384], P('dp', 'fsdp'), may hold values from 0.5 to 50
Outputs:
- projected: bfloat16 [512, 16384], P('dp', 'fsdp')
- normed_gradient_transposed: bfloat16 [16384, 512], P('fsdp', 'dp')
- update_a: float32 [32, 16384, 32], P('dp', 'fsdp')
- update_b: float32 [32, 32, 16384], P('dp', None, 'fsdp')
- row_a_new: float32 [32, 16384], P('dp', 'fsdp')
- col_a_new: float32 [32, 32], P('dp')
- row_b_new: float32 [32, 32], P('dp')
- col_b_new: float32 [32, 16384], P('dp', 'fsdp')
Inputs may be any that keep to these rules, and one draw needn't show every extreme that they name: Distinct slots; tenant t's optimizer state is in slot tenant_slot_index[t], owned by data group tenant_slot_index[t] // 8; every group owns at most 8 tenants and some group owns exactly 8. The first live_row_count[g] rows of data group g are live; some group has all 128 live; the counts sum to 320.
All inputs are finite; a program needn't handle non-finite values.
Results may differ from a plain program's by a relative error of at most 0.0095.
Values may be sent and summed in bfloat16 or wider, within the bound.
No kernel may reach another device: no remote copies, remote signals or barrier semaphores. Data moves between devices by JAX's collectives and lax.ppermute only.
A program may use at most 128 MiB of HBM per device.

v0:
```python
import jax
import jax.numpy as jnp
from jax import lax
from jax.sharding import PartitionSpec as P

ADAPTER_SCALE = 0.5
BETA_TWO = 0.9
SQ_EPS = 1e-30
RMS_EPS = 1e-05


def gather_turned(arrays, axis, dims):
    turned = [jnp.moveaxis(a, dim, 0) for a, dim in zip(arrays, dims)]
    widths = [t[0].size for t in turned]
    both = jnp.concatenate([t.reshape(-1, w) for t, w in zip(turned, widths)], axis=1)
    filled = lax.all_gather(both, axis, axis=0, tiled=True)
    pieces = jnp.split(filled, [sum(widths[:k]) for k in range(1, len(widths))], axis=1)
    return tuple(
        (
            jnp.moveaxis(b.reshape(-1, *t.shape[1:]), 0, dim)
            for b, t, dim in zip(pieces, turned, dims)
        )
    )


def copy_for_each(value, axis):
    copies = jnp.broadcast_to(value, (lax.axis_size(axis), *value.shape))
    return lax.all_to_all(copies, axis, split_axis=0, concat_axis=0, tiled=True)


def of_everyone(value, axis):
    return copy_for_each(value, axis).sum(axis=0)


def over_copies(value, axis):
    return copy_for_each(value, axis).astype(jnp.float32).sum(axis=0)


def together(arrays, axis):
    vector, at, done = (jnp.concatenate([a.reshape(-1) for a in arrays]), 0, [])
    subtotal = of_everyone(vector, axis)
    for a in arrays:
        done.append(subtotal[at : at + a.size].reshape(a.shape))
        at += a.size
    return tuple(done)


def on_device(
    inputs,
    norm_gain_vector,
    weight,
    down_adapters,
    up_adapters,
    tenant,
    tenant_slot_index,
    live_row_count,
    cotangent,
    down_row_factor,
    down_column_factor,
    up_row_factor,
    up_column_factor,
):
    highest_precision = lax.Precision.HIGHEST
    rows, shard_local_width = inputs.shape
    full_width = weight.shape[0]
    tenant_index = down_adapters.shape[1]
    device_rank = down_adapters.shape[2]
    lane = lax.axis_index("fsdp")
    contract_last = (((1,), (1,)), ((), ()))
    contract_first = (((0,), (0,)), ((), ()))
    whole_x, whole_gain = gather_turned((inputs, norm_gain_vector), "fsdp", (1, 0))
    whole_f = whole_x.astype(jnp.float32)
    power = jnp.sum(whole_f * whole_f, axis=1, keepdims=True)
    scale = lax.rsqrt(power / full_width + RMS_EPS)
    normed_full = (whole_f * scale * whole_gain.astype(jnp.float32)).astype(jnp.bfloat16)
    frozen_output = jnp.dot(normed_full, weight, preferred_element_type=jnp.float32)
    normalized_input = lax.dynamic_slice_in_dim(
        normed_full, lane * shard_local_width, shard_local_width, 1
    )
    pick = tenant[:, None] == lax.iota(jnp.int32, tenant_index)[None, :]
    pick_b = pick.astype(jnp.bfloat16)
    pick_f = pick.astype(jnp.float32)
    down_flattened = down_adapters.reshape(shard_local_width, tenant_index * device_rank)
    up_flattened = up_adapters.reshape(tenant_index * device_rank, up_adapters.shape[2])
    inner_all = jnp.dot(normalized_input, down_flattened, preferred_element_type=jnp.float32)
    inner_part = jnp.sum(
        inner_all.reshape(rows, tenant_index, device_rank) * pick_f[:, :, None], axis=1
    )
    inner = of_everyone(inner_part, "fsdp")
    spread_rows = (inner.astype(jnp.bfloat16)[:, None, :] * pick_b[:, :, None]).reshape(
        rows, tenant_index * device_rank
    )
    adapted_output = jnp.dot(spread_rows, up_flattened, preferred_element_type=jnp.float32)
    projected = (frozen_output + ADAPTER_SCALE * adapted_output).astype(jnp.bfloat16)
    live = lax.iota(jnp.int32, rows) < live_row_count[0]
    output_gradient = jnp.where(live[:, None], cotangent, jnp.zeros_like(cotangent))
    back_all = lax.dot_general(
        output_gradient, up_flattened, contract_last, preferred_element_type=jnp.float32
    )
    back_part = jnp.sum(
        back_all.reshape(rows, tenant_index, device_rank) * pick_f[:, :, None], axis=1
    )
    back = of_everyone(back_part, "fsdp")
    backward_spread_rows = (back.astype(jnp.bfloat16)[:, None, :] * pick_b[:, :, None]).reshape(
        rows, tenant_index * device_rank
    )
    frozen_input_gradient = lax.psum_scatter(
        lax.dot_general(weight, output_gradient, contract_last, preferred_element_type=jnp.float32),
        "fsdp",
        scatter_dimension=0,
        tiled=True,
    )
    adapter_input_gradient = lax.dot_general(
        down_flattened, backward_spread_rows, contract_last, preferred_element_type=jnp.float32
    )
    normed_gradient_transposed = (
        frozen_input_gradient + ADAPTER_SCALE * adapter_input_gradient
    ).astype(jnp.bfloat16)
    down_gradient = (
        ADAPTER_SCALE
        * lax.dot_general(
            normalized_input,
            backward_spread_rows,
            contract_first,
            preferred_element_type=jnp.float32,
        )
    ).reshape(shard_local_width, tenant_index, device_rank)
    up_gradient = (
        ADAPTER_SCALE
        * lax.dot_general(
            spread_rows, output_gradient, contract_first, preferred_element_type=jnp.float32
        )
    ).reshape(tenant_index, device_rank, output_gradient.shape[1])
    owned = down_row_factor.shape[0]
    summed_a, summed_b = (
        over_copies(down_gradient.astype(jnp.bfloat16), "dp").astype(jnp.float32),
        over_copies(up_gradient.astype(jnp.bfloat16), "dp").astype(jnp.float32),
    )
    mine = lax.iota(jnp.int32, owned) + lax.axis_index("dp") * owned
    owner_routing = (tenant_slot_index[None, :] == mine[:, None]).astype(jnp.float32)
    ga = jnp.einsum("st,ftr->sfr", owner_routing, summed_a, precision=highest_precision)
    gb = jnp.einsum("ho,oxk->hxk", owner_routing, summed_b, precision=highest_precision)
    sq_a = ga * ga + SQ_EPS
    sq_b = gb * gb + SQ_EPS
    row_a_new = BETA_TWO * down_row_factor + (1.0 - BETA_TWO) * (
        jnp.sum(sq_a, axis=2) / device_rank
    )
    col_b_new = BETA_TWO * up_column_factor + (1.0 - BETA_TWO) * (
        jnp.sum(sq_b, axis=1) / device_rank
    )
    col_sum, rowb_sum, meana_sum = together(
        (jnp.sum(sq_a, axis=1), jnp.sum(sq_b, axis=2), jnp.sum(row_a_new, axis=1)), "fsdp"
    )
    col_a_new = BETA_TWO * down_column_factor + (1.0 - BETA_TWO) * (col_sum / full_width)
    row_b_new = BETA_TWO * up_row_factor + (1.0 - BETA_TWO) * (rowb_sum / full_width)
    mean_a = meana_sum / full_width
    mean_b = jnp.sum(row_b_new, axis=1) / device_rank
    update_a = ga * lax.rsqrt(row_a_new[:, :, None] * col_a_new[:, None, :] / mean_a[:, None, None])
    update_b = gb * lax.rsqrt(row_b_new[:, :, None] * col_b_new[:, None, :] / mean_b[:, None, None])
    return (
        projected,
        normed_gradient_transposed,
        update_a,
        update_b,
        row_a_new,
        col_a_new,
        row_b_new,
        col_b_new,
    )


def solution(mesh):
    return jax.shard_map(
        on_device,
        mesh=mesh,
        in_specs=(
            P("dp", "fsdp"),
            P("fsdp"),
            P(None, "fsdp"),
            P("fsdp", None, None),
            P(None, None, "fsdp"),
            P("dp"),
            P(),
            P("dp"),
            P("dp", "fsdp"),
            P("dp", "fsdp"),
            P("dp", None),
            P("dp", None),
            P("dp", "fsdp"),
        ),
        out_specs=(
            P("dp", "fsdp"),
            P("fsdp", "dp"),
            P("dp", "fsdp", None),
            P("dp", None, "fsdp"),
            P("dp", "fsdp"),
            P("dp", None),
            P("dp", None),
            P("dp", "fsdp"),
        ),
        check_vma=False,
    )
```

profile of v0, /device:TPU:6, one launch (start us, length us, event | category | flops | bytes accessed | tf_op | source)
XLA Modules:
  0.0 264.9 jit_solution(11799860212287939905)
XLA Ops:
  7.2 0.0 copy-start
  7.2 0.0 all-gather.2.cloned.1.call-start
  7.2 1.0 copy.77
  8.2 0.8 reshape.145
  9.0 0.7 pad_maximum_fusion
  9.7 0.0 all-gather.2.cloned.1.call-update
  9.7 0.0 reduce-scatter.2.cloned.1.call-start
  10.4 9.5 %convolution_bitcast_fusion = f32[16384,128]{0,1:T(8,128)} fusion(bf16[16384,256]{1,0:T(8,128)(2,1)} %param.15, bf16[128,256]{1,0:T(8,128)(2,1)} %param.21, pred[128]{0:T(512)(128)(4,1)S(1)} %iota_compare_fusion.1), kind=kOutput, calls=%fused_computation | convolution fusion | flops 1073774592 | bytes 16842880 | tf_op jit(solution)/shard_map/dot_general | solution.py:108
  19.9 0.0 reduce-scatter.2.cloned.1.call-update
  19.9 0.6 copy-done.14
  20.5 0.2 copy-done.3
  20.7 0.3 fusion.6
  21.0 1.1 broadcast_in_dim.23
  22.2 12.1 %all-to-all-start.1 = ((f32[64,128,32]{1,2,0:T(8,128)}), f32[64,128,32]{1,2,0:T(8,128)S(1)}, u32[]{:S(2)}, u32[]{:S(2)}) async-start(f32[64,128,32]{1,2,0:T(8,128)} %broadcast_in_dim.23), calls=%async_computation.2 | async-start | bytes 2097152 | tf_op jit(solution)/shard_map/all_to_all | solution.py:28
  34.3 67.1 %all-gather.2.cloned.1.call-done = bf16[16384,129]{1,0:T(8,128)(2,1)} async-done(((bf16[256,129]{1,0:T(8,128)(2,1)}), bf16[16384,129]{1,0:T(8,128)(2,1)}) %all-gather.2.cloned.1.call-update) | async-done | bytes 4227088 | tf_op jit(solution)/shard_map/all_gather | solution.py:16
  101.3 3.9 %fusion = f32[128]{0:T(128)S(1)} fusion(bf16[16384,129]{1,0:T(8,128)(2,1)} %all-gather.2.cloned.1.call-done), kind=kLoop, calls=%fused_computation.3 | loop fusion | flops 6291328 | bytes 4194816 | tf_op jit(solution)/shard_map/reduce_sum | solution.py:73
  105.3 2.9 %convert_reduce_fusion = f32[16384]{0:T(1024)S(1)} fusion(bf16[16384,129]{1,0:T(8,128)(2,1)} %all-gather.2.cloned.1.call-done), kind=kLoop, calls=%fused_computation.6 | loop fusion | flops 16384 | bytes 98304 | tf_op jit(solution)/shard_map/convert_element_type | solution.py:75
  108.2 6.9 %fusion.2 = bf16[16384,128]{1,0:T(8,128)(2,1)S(1)} fusion(f32[16384]{0:T(1024)S(1)} %convert_reduce_fusion, f32[128]{0:T(128)S(1)} %add_rsqrt_fusion, bf16[16384,129]{1,0:T(8,128)(2,1)S(1)} %copy-done.2), kind=kLoop, calls=%fused_computation.5 | loop fusion | flops 8388608 | bytes 8454656 | tf_op jit(solution)/shard_map/convert_element_type | solution.py:75
  115.1 2.0 copy-done.1
  117.1 0.2 fusion.5
  117.4 1.2 broadcast_in_dim.20
  118.5 6.6 %all-to-all-start = ((f32[64,128,32]{1,2,0:T(8,128)}), f32[64,128,32]{1,2,0:T(8,128)S(1)}, u32[]{:S(2)}, u32[]{:S(2)}) async-start(f32[64,128,32]{1,2,0:T(8,128)} %broadcast_in_dim.20), calls=%async_computation | async-start | bytes 2097152 | tf_op jit(solution)/shard_map/all_to_all | solution.py:28
  125.2 0.1 reduce_sum.130
  125.3 28.8 %all-to-all-done = f32[64,128,32]{1,2,0:T(8,128)S(1)} async-done(((f32[64,128,32]{1,2,0:T(8,128)}), f32[64,128,32]{1,2,0:T(8,128)S(1)}, u32[]{:S(2)}, u32[]{:S(2)}) %all-to-all-start) | async-done | bytes 1048608 | tf_op jit(solution)/shard_map/all_to_all | solution.py:28
  154.1 0.1 reduce_sum.128
  154.2 1.1 fusion.3
  155.3 0.1 copy.79
  155.4 1.2 broadcast_in_dim.24
  156.6 4.6 %all-to-all-start.2 = ((bf16[4,256,16,32]{1,3,2,0:T(8,128)(2,1)}), bf16[4,256,16,32]{1,3,2,0:T(8,128)(2,1)S(1)}, u32[]{:S(2)}, u32[]{:S(2)}) async-start(bf16[4,256,16,32]{1,3,2,0:T(8,128)(2,1)} %broadcast_in_dim.24), calls=%async_computation.3 | async-start | bytes 2097152 | tf_op jit(solution)/shard_map/all_to_all | solution.py:28
  161.2 0.3 fusion.4
  161.5 12.1 %all-to-all-done.2 = bf16[4,256,16,32]{1,3,2,0:T(8,128)(2,1)S(1)} async-done(((bf16[4,256,16,32]{1,3,2,0:T(8,128)(2,1)}), bf16[4,256,16,32]{1,3,2,0:T(8,128)(2,1)S(1)}, u32[]{:S(2)}, u32[]{:S(2)}) %all-to-all-start.2) | async-done | bytes 1048608 | tf_op jit(solution)/shard_map/all_to_all | solution.py:28
  173.6 1.2 broadcast_in_dim.25
  174.8 5.6 %all-to-all-start.3 = ((bf16[4,16,32,256]{3,2,1,0:T(8,128)(2,1)}), bf16[4,16,32,256]{3,2,1,0:T(8,128)(2,1)S(1)}, u32[]{:S(2)}, u32[]{:S(2)}) async-start(bf16[4,16,32,256]{3,2,1,0:T(8,128)(2,1)} %broadcast_in_dim.25), calls=%async_computation.4 | async-start | bytes 2097152 | tf_op jit(solution)/shard_map/all_to_all | solution.py:28
  180.3 0.2 convert_reduce_fusion.2
  180.5 0.7 fusion.19
  181.2 0.1 copy.81
  181.3 0.1 reshape.137
  181.4 10.4 %all-to-all-done.3 = bf16[4,16,32,256]{3,2,1,0:T(8,128)(2,1)S(1)} async-done(((bf16[4,16,32,256]{3,2,1,0:T(8,128)(2,1)}), bf16[4,16,32,256]{3,2,1,0:T(8,128)(2,1)S(1)}, u32[]{:S(2)}, u32[]{:S(2)}) %all-to-all-start.3) | async-done | bytes 1048608 | tf_op jit(solution)/shard_map/all_to_all | solution.py:28
  191.8 0.2 convert_reduce_fusion.1
  191.9 0.7 fusion.21
  192.6 0.1 copy.83
  192.7 0.1 reshape.138
  192.8 0.1 fusion.40
  192.9 0.0 copy-start.5
  192.9 0.8 broadcast_in_dim.26
  193.7 7.1 %all-to-all-start.4 = ((f32[64,1,520]{2,1,0:T(1,128)}), f32[64,1,520]{2,1,0:T(1,128)S(1)}, u32[]{:S(2)}, u32[]{:S(2)}) async-start(f32[64,1,520]{2,1,0:T(1,128)} %broadcast_in_dim.26), calls=%async_computation.5 | async-start | bytes 327680 | tf_op jit(solution)/shard_map/all_to_all | solution.py:28
  200.8 0.0 copy-start.11
  200.8 0.0 copy-start.12
  200.8 6.3 %fusion.41 = f32[128,256]{1,0:T(8,128)S(1)} fusion(bf16[16384,128]{1,0:T(8,128)(2,1)} %copy-done.1, bf16[16384,256]{1,0:T(8,128)(2,1)} %param.15), kind=kOutput, calls=%fused_computation.74 | convolution fusion | flops 1073741824 | bytes 12713984 | tf_op jit(solution)/shard_map/dot_general | solution.py:76
  207.1 0.9 fusion.13
  208.0 5.4 %all-to-all-done.4 = f32[64,1,520]{2,1,0:T(1,128)S(1)} async-done(((f32[64,1,520]{2,1,0:T(1,128)}), f32[64,1,520]{2,1,0:T(1,128)S(1)}, u32[]{:S(2)}, u32[]{:S(2)}) %all-to-all-start.4) | async-done | bytes 133152 | tf_op jit(solution)/shard_map/all_to_all | solution.py:28
  213.4 0.1 reduce_sum.137
  213.5 0.1 mul.211
  213.6 0.1 fusion.39
  213.7 0.1 copy.86
  213.8 0.1 rsqrt_multiply_fusion
  213.9 0.8 copy.89
  214.7 0.1 mul.205
  214.8 0.1 copy.85
  214.9 0.1 rsqrt_multiply_fusion.1
  215.0 0.8 copy.88
  215.8 40.4 %reduce-scatter.2.cloned.1.call-done = f32[256,128]{0,1:T(8,128)} async-done(((f32[16384,128]{0,1:T(8,128)}), f32[256,128]{0,1:T(8,128)}) %reduce-scatter.2.cloned.1.call-update) | async-done | bytes 131088 | tf_op jit(solution)/shard_map/reduce_scatter | solution.py:107
  256.2 1.1 fusion.12
  257.4 0.7 copy.87
  (34 shorter events, 0.1 us)
Async XLA Ops:
  7.2 13.4 %copy-start = (bf16[16,32,256]{2,1,0:T(8,128)(2,1)S(1)}, bf16[16,32,256]{2,1,0:T(8,128)(2,1)}, u32[]{:S(2)}) copy-start(bf16[16,32,256]{2,1,0:T(8,128)(2,1)} %param.17) | copy-start | bytes 786436
  7.2 94.1 %all-gather.2.cloned.1.call-start = ((), (), s32[]{:S(2)}) async-start(), calls=%async_computation.6 | async-start | bytes 8519680 | tf_op jit(solution)/shard_map/all_gather | solution.py:16
  9.7 246.5 %reduce-scatter.2.cloned.1.call-start = ((), (), s32[]{:S(2)}) async-start(), calls=%async_computation.7 | async-start | bytes 8519680 | tf_op jit(solution)/shard_map/reduce_scatter | solution.py:107
  19.9 0.7 copy-start.14
  19.9 0.9 copy-start.3
  22.2 95.2 %all-to-all-start.1 = ((f32[64,128,32]{1,2,0:T(8,128)}), f32[64,128,32]{1,2,0:T(8,128)S(1)}, u32[]{:S(2)}, u32[]{:S(2)}) async-start(f32[64,128,32]{1,2,0:T(8,128)} %broadcast_in_dim.23), calls=%async_computation.2 | async-start | bytes 2097152 | tf_op jit(solution)/shard_map/all_to_all | solution.py:28
  101.3 6.8 %copy-start.2 = (bf16[16384,129]{1,0:T(8,128)(2,1)S(1)}, bf16[16384,129]{1,0:T(8,128)(2,1)}, u32[]{:S(2)}) copy-start(bf16[16384,129]{1,0:T(8,128)(2,1)} %all-gather.2.cloned.1.call-done) | copy-start | bytes 12681220
  101.3 15.8 %copy-start.4 = (bf16[256,16,32]{0,2,1:T(8,128)(2,1)S(1)}, bf16[256,16,32]{0,2,1:T(8,128)(2,1)}, u32[]{:S(2)}) copy-start(bf16[256,16,32]{0,2,1:T(8,128)(2,1)} %param.16) | copy-start | bytes 786436
  115.1 2.0 copy-start.1
  117.1 63.4 %copy-start.13 = (s32[16]{0:T(128)S(1)}, s32[16]{0:T(128)}, u32[]{:S(2)}) copy-start(s32[16]{0:T(128)} %param.19) | copy-start | bytes 196
  118.5 74.2 %copy-start.9 = (f32[8,256]{1,0:T(8,128)S(1)}, f32[8,256]{1,0:T(8,128)}, u32[]{:S(2)}) copy-start(f32[8,256]{1,0:T(8,128)} %param.22) | copy-start | bytes 24580
  118.5 74.2 %copy-start.10 = (f32[8,256]{1,0:T(8,128)S(1)}, f32[8,256]{1,0:T(8,128)}, u32[]{:S(2)}) copy-start(f32[8,256]{1,0:T(8,128)} %param.25) | copy-start | bytes 24580
  118.5 35.5 %all-to-all-start = ((f32[64,128,32]{1,2,0:T(8,128)}), f32[64,128,32]{1,2,0:T(8,128)S(1)}, u32[]{:S(2)}, u32[]{:S(2)}) async-start(f32[64,128,32]{1,2,0:T(8,128)} %broadcast_in_dim.20), calls=%async_computation | async-start | bytes 2097152 | tf_op jit(solution)/shard_map/all_to_all | solution.py:28
  156.6 17.0 %all-to-all-start.2 = ((bf16[4,256,16,32]{1,3,2,0:T(8,128)(2,1)}), bf16[4,256,16,32]{1,3,2,0:T(8,128)(2,1)S(1)}, u32[]{:S(2)}, u32[]{:S(2)}) async-start(bf16[4,256,16,32]{1,3,2,0:T(8,128)(2,1)} %broadcast_in_dim.24), calls=%async_computation.3 | async-start | bytes 2097152 | tf_op jit(solution)/shard_map/all_to_all | solution.py:28
  174.8 17.0 %all-to-all-start.3 = ((bf16[4,16,32,256]{3,2,1,0:T(8,128)(2,1)}), bf16[4,16,32,256]{3,2,1,0:T(8,128)(2,1)S(1)}, u32[]{:S(2)}, u32[]{:S(2)}) async-start(bf16[4,16,32,256]{3,2,1,0:T(8,128)(2,1)} %broadcast_in_dim.25), calls=%async_computation.4 | async-start | bytes 2097152 | tf_op jit(solution)/shard_map/all_to_all | solution.py:28
  192.9 20.9 %copy-start.6 = (f32[8,256]{1,0:T(8,128)}, f32[8,256]{1,0:T(8,128)S(1)}, u32[]{:S(2)}) copy-start(f32[8,256]{1,0:T(8,128)S(1)} %get-tuple-element.80) | copy-start | bytes 24580
  192.9 22.0 %copy-start.5 = (f32[8,256]{1,0:T(8,128)}, f32[8,256]{1,0:T(8,128)S(1)}, u32[]{:S(2)}) copy-start(f32[8,256]{1,0:T(8,128)S(1)} %get-tuple-element.71) | copy-start | bytes 24580
  193.7 19.7 %all-to-all-start.4 = ((f32[64,1,520]{2,1,0:T(1,128)}), f32[64,1,520]{2,1,0:T(1,128)S(1)}, u32[]{:S(2)}, u32[]{:S(2)}) async-start(f32[64,1,520]{2,1,0:T(1,128)} %broadcast_in_dim.26), calls=%async_computation.5 | async-start | bytes 327680 | tf_op jit(solution)/shard_map/all_to_all | solution.py:28
  200.8 12.8 %copy-start.11 = (f32[8,32]{1,0:T(8,128)S(1)}, f32[8,32]{1,0:T(8,128)}, u32[]{:S(2)}) copy-start(f32[8,32]{1,0:T(8,128)} %param.24) | copy-start | bytes 3076
  200.8 14.0 %copy-start.12 = (f32[8,32]{1,0:T(8,128)S(1)}, f32[8,32]{1,0:T(8,128)}, u32[]{:S(2)}) copy-start(f32[8,32]{1,0:T(8,128)} %param.23) | copy-start | bytes 3076
  213.7 44.4 %copy-start.7 = (f32[8,32]{1,0:T(8,128)}, f32[8,32]{1,0:T(8,128)S(1)}, u32[]{:S(2)}) copy-start(f32[8,32]{1,0:T(8,128)S(1)} %get-tuple-element.69) | copy-start | bytes 3076
  214.8 43.3 %copy-start.8 = (f32[8,32]{1,0:T(8,128)}, f32[8,32]{1,0:T(8,128)S(1)}, u32[]{:S(2)}) copy-start(f32[8,32]{1,0:T(8,128)S(1)} %multiply_add_fusion.5) | copy-start | bytes 3076
Sparse Core Ops, SparseCore 0:
  11.4 89.9 all-gather.1
  105.5 150.6 reduce-scatter.1
where the time goes:
time: 266 us; the launch traced here: 265 us
  waiting for transfers between devices  164 us (62%)
  starting transfers between devices  36.1 us (14%)
  matrix products  21 us (8%)
  other arithmetic  15.7 us (6%)
  between operations  15 us (6%)
  local copies, waits for them, and re-layouts  13 us (5%)
    all_gather x1, waiting for transfers between devices, gather_turned(): filled = lax.all_gather(both, axis, axis=0, tiled=True)  67.1 us
    all_to_all x5, waiting for transfers between devices, copy_for_each(): return lax.all_to_all(copies, axis, split_axis=0, concat_axis=0, tiled=True)  56.6 us
    reduce_scatter x1, waiting for transfers between devices, on_device(): lax.psum_scatter(lax.dot_general(weight, output_gradient, contract_last,...  40.4 us
    all_to_all x5, starting transfers between devices, copy_for_each(): return lax.all_to_all(copies, axis, split_axis=0, concat_axis=0, tiled=True)  36 us
    dot_general x1, matrix products, on_device(): lax.dot_general(weight, output_gradient, contract_last, preferred_element...  9.48 us
    convert_element_type x1, other arithmetic, on_device(): (whole_f * scale * whole_gain.astype(jnp.float32)).astype(jnp.bfloat16)  6.95 us
    dot_general x1, matrix products, on_device(): jnp.dot(normed_full, weight, preferred_element_type=jnp.float32)  6.28 us
    unnamed x34, local copies, waits for them, and re-layouts  6.13 us
  transfers between devices with their start and end apart: 7, of which 6 were waited for; matrix products, arithmetic and copies ran while one was open for 16% of the time, Pallas kernels for 0%

commit v1 on v0

--- a/solution.py
+++ b/solution.py
@@ -13,7 +13,10 @@
     turned = [jnp.moveaxis(a, dim, 0) for a, dim in zip(arrays, dims)]
     widths = [t[0].size for t in turned]
     both = jnp.concatenate([t.reshape(-1, w) for t, w in zip(turned, widths)], axis=1)
-    filled = lax.all_gather(both, axis, axis=0, tiled=True)
+    size = lax.axis_size(axis)
+    parts = jnp.stack([both for _ in range(size)])
+    parts = lax.all_to_all(parts, axis, split_axis=0, concat_axis=0)
+    filled = jnp.concatenate(parts, axis=0)
     pieces = jnp.split(filled, [sum(widths[:k]) for k in range(1, len(widths))], axis=1)
     return tuple(
         (

time: 266 us -> 284 us (1.068)
  local copies, waits for them, and re-layouts: 13 us -> 23.7 us
  starting transfers between devices: 36.1 us -> 42.9 us
    all_to_all x0 -> x1, waiting for transfers between devices: none -> 93.5 us  [gather_turned(): parts = lax.all_to_all(parts, axis, split_axis=0, concat_axis=0)]
    all_gather x1 -> x0, waiting for transfers between devices: 67.1 us -> none  [gather_turned(): filled = lax.all_gather(both, axis, axis=0, tiled=True)]
    reduce_scatter x1, waiting for transfers between devices: 40.4 us -> 0.01 us  [on_device(): lax.psum_scatter(lax.dot_general(weight, output_gradient, contract_last,...]
    all_to_all x0 -> x1, starting transfers between devices: none -> 12.3 us  [gather_turned(): parts = lax.all_to_all(parts, axis, split_axis=0, concat_axis=0)]
    all_to_all x5, waiting for transfers between devices: 56.6 us -> 68.9 us  [copy_for_each(): return lax.all_to_all(copies, axis, split_axis=0, concat_axis=0, tiled=True)]
    all_to_all x0 -> x1, local copies, waits for them, and re-layouts: none -> 9.53 us  [gather_turned(): parts = lax.all_to_all(parts, axis, split_axis=0, concat_axis=0)]
    all_to_all x5, starting transfers between devices: 36 us -> 30.5 us  [copy_for_each(): return lax.all_to_all(copies, axis, split_axis=0, concat_axis=0, tiled=True)]
    unnamed x34 -> x33, local copies, waits for them, and re-layouts: 6.13 us -> 4.97 us
  transfers between devices with their start and end apart: 7 -> 7, of which waited for: 6 -> 6; matrix products, arithmetic and copies ran while one was open for 16% -> 19% of each run, Pallas kernels for 0% -> 0%
where the time goes in v1:
time: 284 us; the launch traced here: 281 us
  waiting for transfers between devices  162 us (57%)
  starting transfers between devices  42.9 us (15%)
  local copies, waits for them, and re-layouts  23.7 us (8%)
  matrix products  20.9 us (7%)
  other arithmetic  15.8 us (6%)
  between operations  14.9 us (5%)
    all_to_all x1, waiting for transfers between devices, gather_turned(): parts = lax.all_to_all(parts, axis, split_axis=0, concat_axis=0)  93.5 us
    all_to_all x5, waiting for transfers between devices, copy_for_each(): return lax.all_to_all(copies, axis, split_axis=0, concat_axis=0, tiled=True)  68.9 us
    all_to_all x5, starting transfers between devices, copy_for_each(): return lax.all_to_all(copies, axis, split_axis=0, concat_axis=0, tiled=True)  30.5 us
    all_to_all x1, starting transfers between devices, gather_turned(): parts = lax.all_to_all(parts, axis, split_axis=0, concat_axis=0)  12.3 us
    all_to_all x1, local copies, waits for them, and re-layouts, gather_turned(): parts = lax.all_to_all(parts, axis, split_axis=0, concat_axis=0)  9.53 us
    dot_general x1, matrix products, on_device(): lax.dot_general(weight, output_gradient, contract_last, preferred_element...  9.44 us
    convert_element_type x1, other arithmetic, on_device(): (whole_f * scale * whole_gain.astype(jnp.float32)).astype(jnp.bfloat16)  6.95 us
    dot_general x1, matrix products, on_device(): jnp.dot(normed_full, weight, preferred_element_type=jnp.float32)  6.19 us
  transfers between devices with their start and end apart: 7, of which 6 were waited for; matrix products, arithmetic and copies ran while one was open for 19% of the time, Pallas kernels for 0%

profile of v1, /device:TPU:6, one launch (start us, length us, event | category | flops | bytes accessed | tf_op | source)
XLA Modules:
  0.0 280.6 jit_solution(1399471838292364018)
XLA Ops:
  7.2 0.0 copy-start
  7.2 0.7 reshape.140
  7.9 0.8 pad_maximum_fusion
  8.8 2.3 stack.2
  11.1 12.3 %all-to-all-start = ((bf16[64,256,129]{1,2,0:T(8,128)(2,1)}), bf16[64,256,129]{1,2,0:T(8,128)(2,1)}, u32[]{:S(2)}, u32[]{:S(2)}) async-start(bf16[64,256,129]{1,2,0:T(8,128)(2,1)} %stack.2), calls=%async_computation | async-start | bytes 8912896 | tf_op jit(solution)/shard_map/all_to_all | solution.py:18
  23.4 0.0 reduce-scatter.2.cloned.1.call-start
  24.2 9.4 %convolution_bitcast_fusion = f32[16384,128]{0,1:T(8,128)} fusion(bf16[16384,256]{1,0:T(8,128)(2,1)} %param.15, bf16[128,256]{1,0:T(8,128)(2,1)S(1)} %copy-done.3, pred[128]{0:T(512)(128)(4,1)S(1)} %iota_compare_fusion.1), kind=kOutput, calls=%fused_computation | convolution fusion | flops 1073774592 | bytes 16842880 | tf_op jit(solution)/shard_map/dot_general | solution.py:111
  33.6 0.0 reduce-scatter.2.cloned.1.call-update
  33.6 0.6 copy-done.14
  34.3 0.3 fusion.6
  34.6 93.5 %all-to-all-done = bf16[64,256,129]{1,2,0:T(8,128)(2,1)} async-done(((bf16[64,256,129]{1,2,0:T(8,128)(2,1)}), bf16[64,256,129]{1,2,0:T(8,128)(2,1)}, u32[]{:S(2)}, u32[]{:S(2)}) %all-to-all-start) | async-done | bytes 4227104 | tf_op jit(solution)/shard_map/all_to_all | solution.py:18
  128.1 1.1 broadcast_in_dim.23
  129.2 6.1 %all-to-all-start.2 = ((f32[64,128,32]{1,2,0:T(8,128)}), f32[64,128,32]{1,2,0:T(8,128)S(1)}, u32[]{:S(2)}, u32[]{:S(2)}) async-start(f32[64,128,32]{1,2,0:T(8,128)} %broadcast_in_dim.23), calls=%async_computation.3 | async-start | bytes 2097152 | tf_op jit(solution)/shard_map/all_to_all | solution.py:31
  135.3 9.5 %copy.72 = bf16[64,256,129]{2,1,0:T(8,128)(2,1)} copy(bf16[64,256,129]{1,2,0:T(8,128)(2,1)} %all-to-all-done) | data formatting | bytes 8454144 | tf_op jit(solution)/shard_map/all_to_all | solution.py:18
  144.9 3.9 %fusion = f32[128]{0:T(128)S(1)} fusion(bf16[16384,129]{1,0:T(8,128)(2,1)} %bitcast.64), kind=kLoop, calls=%fused_computation.3 | loop fusion | flops 6291328 | bytes 4194816 | tf_op jit(solution)/shard_map/reduce_sum | solution.py:76
  148.8 2.9 %convert_reduce_fusion = f32[16384]{0:T(1024)S(1)} fusion(bf16[16384,129]{1,0:T(8,128)(2,1)} %bitcast.65), kind=kLoop, calls=%fused_computation.6 | loop fusion | flops 16384 | bytes 98304 | tf_op jit(solution)/shard_map/convert_element_type | solution.py:78
  151.7 6.9 %fusion.2 = bf16[16384,128]{1,0:T(8,128)(2,1)S(1)} fusion(f32[16384]{0:T(1024)S(1)} %convert_reduce_fusion, f32[128]{0:T(128)S(1)} %add_rsqrt_fusion, bf16[16384,129]{1,0:T(8,128)(2,1)S(1)} %bitcast.66), kind=kLoop, calls=%fused_computation.5 | loop fusion | flops 8388608 | bytes 8454656 | tf_op jit(solution)/shard_map/convert_element_type | solution.py:78
  158.7 2.0 copy-done.2
  160.7 0.2 fusion.5
  160.9 8.8 %all-to-all-done.2 = f32[64,128,32]{1,2,0:T(8,128)S(1)} async-done(((f32[64,128,32]{1,2,0:T(8,128)}), f32[64,128,32]{1,2,0:T(8,128)S(1)}, u32[]{:S(2)}, u32[]{:S(2)}) %all-to-all-start.2) | async-done | bytes 1048608 | tf_op jit(solution)/shard_map/all_to_all | solution.py:31
  169.7 1.2 broadcast_in_dim.20
  170.9 7.6 %all-to-all-start.1 = ((f32[64,128,32]{1,2,0:T(8,128)}), f32[64,128,32]{1,2,0:T(8,128)S(1)}, u32[]{:S(2)}, u32[]{:S(2)}) async-start(f32[64,128,32]{1,2,0:T(8,128)} %broadcast_in_dim.20), calls=%async_computation.1 | async-start | bytes 2097152 | tf_op jit(solution)/shard_map/all_to_all | solution.py:31
  178.5 0.1 reduce_sum.130
  178.6 32.9 %all-to-all-done.1 = f32[64,128,32]{1,2,0:T(8,128)S(1)} async-done(((f32[64,128,32]{1,2,0:T(8,128)}), f32[64,128,32]{1,2,0:T(8,128)S(1)}, u32[]{:S(2)}, u32[]{:S(2)}) %all-to-all-start.1) | async-done | bytes 1048608 | tf_op jit(solution)/shard_map/all_to_all | solution.py:31
  211.5 0.1 reduce_sum.128
  211.7 0.3 fusion.4
  211.9 1.2 broadcast_in_dim.25
  213.1 4.7 %all-to-all-start.4 = ((bf16[4,16,32,256]{3,2,1,0:T(8,128)(2,1)}), bf16[4,16,32,256]{3,2,1,0:T(8,128)(2,1)S(1)}, u32[]{:S(2)}, u32[]{:S(2)}) async-start(bf16[4,16,32,256]{3,2,1,0:T(8,128)(2,1)} %broadcast_in_dim.25), calls=%async_computation.5 | async-start | bytes 2097152 | tf_op jit(solution)/shard_map/all_to_all | solution.py:31
  217.8 1.1 fusion.3
  218.9 0.1 copy.73
  219.0 11.7 %all-to-all-done.4 = bf16[4,16,32,256]{3,2,1,0:T(8,128)(2,1)S(1)} async-done(((bf16[4,16,32,256]{3,2,1,0:T(8,128)(2,1)}), bf16[4,16,32,256]{3,2,1,0:T(8,128)(2,1)S(1)}, u32[]{:S(2)}, u32[]{:S(2)}) %all-to-all-start.4) | async-done | bytes 1048608 | tf_op jit(solution)/shard_map/all_to_all | solution.py:31
  230.7 1.2 broadcast_in_dim.24
  231.9 5.6 %all-to-all-start.3 = ((bf16[4,256,16,32]{1,3,2,0:T(8,128)(2,1)}), bf16[4,256,16,32]{1,3,2,0:T(8,128)(2,1)S(1)}, u32[]{:S(2)}, u32[]{:S(2)}) async-start(bf16[4,256,16,32]{1,3,2,0:T(8,128)(2,1)} %broadcast_in_dim.24), calls=%async_computation.4 | async-start | bytes 2097152 | tf_op jit(solution)/shard_map/all_to_all | solution.py:31
  237.5 0.2 convert_reduce_fusion.1
  237.7 0.7 fusion.21
  238.4 0.1 copy.77
  238.4 0.1 reshape.144
  238.5 10.9 %all-to-all-done.3 = bf16[4,256,16,32]{1,3,2,0:T(8,128)(2,1)S(1)} async-done(((bf16[4,256,16,32]{1,3,2,0:T(8,128)(2,1)}), bf16[4,256,16,32]{1,3,2,0:T(8,128)(2,1)S(1)}, u32[]{:S(2)}, u32[]{:S(2)}) %all-to-all-start.3) | async-done | bytes 1048608 | tf_op jit(solution)/shard_map/all_to_all | solution.py:31
  249.4 0.2 convert_reduce_fusion.2
  249.6 0.7 fusion.19
  250.3 0.1 copy.75
  250.4 0.1 reshape.143
  250.5 0.1 fusion.40
  250.6 0.0 copy-start.5
  250.6 0.0 copy-start.6
  250.6 0.8 broadcast_in_dim.26
  251.4 6.5 %all-to-all-start.5 = ((f32[64,1,520]{2,1,0:T(1,128)}), f32[64,1,520]{2,1,0:T(1,128)S(1)}, u32[]{:S(2)}, u32[]{:S(2)}) async-start(f32[64,1,520]{2,1,0:T(1,128)} %broadcast_in_dim.26), calls=%async_computation.6 | async-start | bytes 327680 | tf_op jit(solution)/shard_map/all_to_all | solution.py:31
  257.9 0.0 copy-start.11
  257.9 0.0 copy-start.12
  257.9 6.2 %fusion.41 = f32[128,256]{1,0:T(8,128)S(1)} fusion(bf16[16384,128]{1,0:T(8,128)(2,1)} %copy-done.2, bf16[16384,256]{1,0:T(8,128)(2,1)} %param.15), kind=kOutput, calls=%fused_computation.74 | convolution fusion | flops 1073741824 | bytes 12713984 | tf_op jit(solution)/shard_map/dot_general | solution.py:79
  264.1 0.9 fusion.13
  264.9 4.5 %all-to-all-done.5 = f32[64,1,520]{2,1,0:T(1,128)S(1)} async-done(((f32[64,1,520]{2,1,0:T(1,128)}), f32[64,1,520]{2,1,0:T(1,128)S(1)}, u32[]{:S(2)}, u32[]{:S(2)}) %all-to-all-start.5) | async-done | bytes 133152 | tf_op jit(solution)/shard_map/all_to_all | solution.py:31
  269.5 0.1 reduce_sum.137
  269.6 0.1 mul.205
  269.7 0.1 copy.79
  269.8 0.1 rsqrt_multiply_fusion.1
  269.9 0.8 copy.82
  270.7 0.1 mul.211
  270.8 0.1 fusion.39
  270.9 0.1 copy.80
  271.0 0.1 rsqrt_multiply_fusion
  271.1 0.8 copy.83
  271.9 1.1 fusion.12
  273.0 0.7 copy.81
  (34 shorter events, 0.1 us)
Async XLA Ops:
  7.2 27.1 %copy-start = (bf16[16,32,256]{2,1,0:T(8,128)(2,1)S(1)}, bf16[16,32,256]{2,1,0:T(8,128)(2,1)}, u32[]{:S(2)}) copy-start(bf16[16,32,256]{2,1,0:T(8,128)(2,1)} %param.17) | copy-start | bytes 786436
  7.2 17.0 %copy-start.3 = (bf16[128,256]{1,0:T(8,128)(2,1)S(1)}, bf16[128,256]{1,0:T(8,128)(2,1)}, u32[]{:S(2)}) copy-start(bf16[128,256]{1,0:T(8,128)(2,1)} %param.21) | copy-start | bytes 196612
  11.1 117.0 %all-to-all-start = ((bf16[64,256,129]{1,2,0:T(8,128)(2,1)}), bf16[64,256,129]{1,2,0:T(8,128)(2,1)}, u32[]{:S(2)}, u32[]{:S(2)}) async-start(bf16[64,256,129]{1,2,0:T(8,128)(2,1)} %stack.2), calls=%async_computation | async-start | bytes 8912896 | tf_op jit(solution)/shard_map/all_to_all | solution.py:18
  23.4 248.5 %reduce-scatter.2.cloned.1.call-start = ((), (), s32[]{:S(2)}) async-start(), calls=%async_computation.7 | async-start | bytes 8519680 | tf_op jit(solution)/shard_map/reduce_scatter | solution.py:110
  33.6 0.7 copy-start.14
  129.2 40.5 %all-to-all-start.2 = ((f32[64,128,32]{1,2,0:T(8,128)}), f32[64,128,32]{1,2,0:T(8,128)S(1)}, u32[]{:S(2)}, u32[]{:S(2)}) async-start(f32[64,128,32]{1,2,0:T(8,128)} %broadcast_in_dim.23), calls=%async_computation.3 | async-start | bytes 2097152 | tf_op jit(solution)/shard_map/all_to_all | solution.py:31
  144.9 6.8 %copy-start.1 = (bf16[64,256,129]{2,1,0:T(8,128)(2,1)S(1)}, bf16[64,256,129]{2,1,0:T(8,128)(2,1)}, u32[]{:S(2)}) copy-start(bf16[64,256,129]{2,1,0:T(8,128)(2,1)} %copy.72) | copy-start | bytes 12681220
  144.9 15.8 %copy-start.4 = (bf16[256,16,32]{0,2,1:T(8,128)(2,1)S(1)}, bf16[256,16,32]{0,2,1:T(8,128)(2,1)}, u32[]{:S(2)}) copy-start(bf16[256,16,32]{0,2,1:T(8,128)(2,1)} %param.16) | copy-start | bytes 786436
  158.7 2.0 copy-start.2
  160.7 77.0 %copy-start.13 = (s32[16]{0:T(128)S(1)}, s32[16]{0:T(128)}, u32[]{:S(2)}) copy-start(s32[16]{0:T(128)} %param.19) | copy-start | bytes 196
  170.9 79.6 %copy-start.9 = (f32[8,256]{1,0:T(8,128)S(1)}, f32[8,256]{1,0:T(8,128)}, u32[]{:S(2)}) copy-start(f32[8,256]{1,0:T(8,128)} %param.22) | copy-start | bytes 24580
  170.9 79.6 %copy-start.10 = (f32[8,256]{1,0:T(8,128)S(1)}, f32[8,256]{1,0:T(8,128)}, u32[]{:S(2)}) copy-start(f32[8,256]{1,0:T(8,128)} %param.25) | copy-start | bytes 24580
  170.9 40.6 %all-to-all-start.1 = ((f32[64,128,32]{1,2,0:T(8,128)}), f32[64,128,32]{1,2,0:T(8,128)S(1)}, u32[]{:S(2)}, u32[]{:S(2)}) async-start(f32[64,128,32]{1,2,0:T(8,128)} %broadcast_in_dim.20), calls=%async_computation.1 | async-start | bytes 2097152 | tf_op jit(solution)/shard_map/all_to_all | solution.py:31
  213.1 17.6 %all-to-all-start.4 = ((bf16[4,16,32,256]{3,2,1,0:T(8,128)(2,1)}), bf16[4,16,32,256]{3,2,1,0:T(8,128)(2,1)S(1)}, u32[]{:S(2)}, u32[]{:S(2)}) async-start(bf16[4,16,32,256]{3,2,1,0:T(8,128)(2,1)} %broadcast_in_dim.25), calls=%async_computation.5 | async-start | bytes 2097152 | tf_op jit(solution)/shard_map/all_to_all | solution.py:31
  231.9 17.5 %all-to-all-start.3 = ((bf16[4,256,16,32]{1,3,2,0:T(8,128)(2,1)}), bf16[4,256,16,32]{1,3,2,0:T(8,128)(2,1)S(1)}, u32[]{:S(2)}, u32[]{:S(2)}) async-start(bf16[4,256,16,32]{1,3,2,0:T(8,128)(2,1)} %broadcast_in_dim.24), calls=%async_computation.4 | async-start | bytes 2097152 | tf_op jit(solution)/shard_map/all_to_all | solution.py:31
  250.6 19.2 %copy-start.5 = (f32[8,256]{1,0:T(8,128)}, f32[8,256]{1,0:T(8,128)S(1)}, u32[]{:S(2)}) copy-start(f32[8,256]{1,0:T(8,128)S(1)} %get-tuple-element.71) | copy-start | bytes 24580
  250.6 20.4 %copy-start.6 = (f32[8,256]{1,0:T(8,128)}, f32[8,256]{1,0:T(8,128)S(1)}, u32[]{:S(2)}) copy-start(f32[8,256]{1,0:T(8,128)S(1)} %get-tuple-element.80) | copy-start | bytes 24580
  251.4 18.1 %all-to-all-start.5 = ((f32[64,1,520]{2,1,0:T(1,128)}), f32[64,1,520]{2,1,0:T(1,128)S(1)}, u32[]{:S(2)}, u32[]{:S(2)}) async-start(f32[64,1,520]{2,1,0:T(1,128)} %broadcast_in_dim.26), calls=%async_computation.6 | async-start | bytes 327680 | tf_op jit(solution)/shard_map/all_to_all | solution.py:31
  257.9 11.8 %copy-start.11 = (f32[8,32]{1,0:T(8,128)S(1)}, f32[8,32]{1,0:T(8,128)}, u32[]{:S(2)}) copy-start(f32[8,32]{1,0:T(8,128)} %param.23) | copy-start | bytes 3076
  257.9 12.9 %copy-start.12 = (f32[8,32]{1,0:T(8,128)S(1)}, f32[8,32]{1,0:T(8,128)}, u32[]{:S(2)}) copy-start(f32[8,32]{1,0:T(8,128)} %param.24) | copy-start | bytes 3076
  269.7 4.1 %copy-start.7 = (f32[8,32]{1,0:T(8,128)}, f32[8,32]{1,0:T(8,128)S(1)}, u32[]{:S(2)}) copy-start(f32[8,32]{1,0:T(8,128)S(1)} %multiply_add_fusion.5) | copy-start | bytes 3076
  270.9 2.9 %copy-start.8 = (f32[8,32]{1,0:T(8,128)}, f32[8,32]{1,0:T(8,128)S(1)}, u32[]{:S(2)}) copy-start(f32[8,32]{1,0:T(8,128)S(1)} %get-tuple-element.69) | copy-start | bytes 3076
Sparse Core Ops, SparseCore 0:
  33.7 177.2 reduce-scatter.1
